TPU v7x, 32 devices: a whole 2x2x4 slice. The times are simulated.
32 devices in a mesh: ind: 16 (over z, y, core), slab: 2 (over x).
Axes of the slice: x: 2, y: 2, z: 4, core: 2. Of those that a mesh axis runs over, the one named last changes fastest.
Arguments:
- dosages: float32 [8192, 2048], P('ind', 'slab'), may hold values from 0 to 2
- tile_rows: int32 [256], P('ind'), may hold values from -1 to 15, as said below
- tile_cols: int32 [256], P('ind'), may hold values from -1 to 15, as said below
Outputs:
- allele_freq: float32 [2048], P('slab')
- grm_tiles: float32 [256, 512, 512], P(('ind', 'slab'))
Inputs may be any that keep to these rules, and one draw needn't show every extreme that they name: `tile_rows`: slots s * 16 to (s + 1) * 16 - 1 belong to owner s. An owner's listed tiles fill its first slots and the rest are -1; every owner lists 2 or more tiles, and some owner fills all 16 slots in every draw. `tile_cols`: -1 exactly where tile_rows is -1; elsewhere not below tile_rows at the same slot.
All inputs are finite; a program needn't handle non-finite values.
Results may differ from a plain program's by a relative error of at most 0.0011.
Values may be sent and summed in bfloat16 or wider, within the bound.
A program may use at most 128 MiB of HBM per device.

v0:
```python
import jax
import jax.numpy as jnp
from jax import lax
from jax.sharding import PartitionSpec as P

VARIANTS = 2048


def standardize(dosages):
    local_sum = jnp.sum(dosages, axis=0)
    total_sum = lax.psum(local_sum, "ind")
    people = dosages.shape[0] * lax.axis_size("ind")
    allele_freq = total_sum / (2.0 * people)
    spread = jnp.maximum(2.0 * allele_freq * (1.0 - allele_freq), 0.05)
    standard = ((dosages - 2.0 * allele_freq) * lax.rsqrt(spread)).astype(jnp.bfloat16)
    return (allele_freq, standard)


def per_device(dosages, tile_rows, tile_cols):
    allele_freq, standard = standardize(dosages)
    block_rows = standard.shape[0]
    variant_dev = standard.shape[1]
    gathered = lax.all_gather(standard, "ind", axis=0, tiled=True)
    groups = gathered.reshape(-1, block_rows, variant_dev)
    row_blocks = groups[jnp.maximum(tile_rows, 0)]
    col_blocks = groups[jnp.maximum(tile_cols, 0)]
    slab_count = lax.axis_size("slab")
    per_slab = tile_rows.shape[0] // slab_count
    own_first = lax.axis_index("slab") * per_slab
    listed = lax.dynamic_slice_in_dim(tile_rows, own_first, per_slab, 0) >= 0
    summed = lax.psum_scatter(
        jnp.einsum("krv,kcv->krc", row_blocks, col_blocks, preferred_element_type=jnp.float32),
        "slab",
        scatter_dimension=0,
        tiled=True,
    )
    grm_tiles = jnp.where(listed[:, None, None], summed / VARIANTS, jnp.float32(0.0))
    return (allele_freq, grm_tiles)


def solution(mesh):
    in_specs = (P("ind", "slab"), P("ind"), P("ind"))
    out_specs = (P("slab"), P(("ind", "slab"), None, None))
    return jax.shard_map(
        per_device, mesh=mesh, in_specs=in_specs, out_specs=out_specs, check_vma=False
    )
```

profile of v0, /device:TPU:0, one launch (start us, length us, event | category | flops | bytes accessed | tf_op | source)
XLA Modules:
  0.0 421.8 jit_solution(15888573012356844928)
XLA Ops:
  7.2 0.0 all-gather.2.cloned.1.call-start
  7.2 1.7 reduce_sum.9
  8.9 34.9 %psum.7 = f32[1024]{0:T(1024)S(1)} all-reduce(f32[1024]{0:T(1024)S(1)} %reduce_sum.9), channel_id=1, replica_groups=mesh['ind'=16,'slab'=2] {'ind'}, use_global_device_ids=true, to_apply=%region_1.0 | all-reduce | flops 1024 | bytes 8192 | tf_op jit(solution)/shard_map/psum | solution.py:11
  43.9 0.6 maximum_rsqrt_fusion
  44.5 2.8 multiply_convert_fusion
  47.3 0.0 all-gather.2.cloned.1.call-update
  47.3 0.0 reduce-scatter.2.cloned.1.call-start
  47.4 0.7 broadcast_maximum_fusion.1
  48.1 0.7 broadcast_maximum_fusion
  48.7 122.9 %all-gather.2.cloned.1.call-done = bf16[8192,1024]{1,0:T(8,128)(2,1)} async-done(((bf16[512,1024]{1,0:T(8,128)(2,1)}), bf16[8192,1024]{1,0:T(8,128)(2,1)}) %all-gather.2.cloned.1.call-update) | async-done | bytes 16777232 | tf_op jit(solution)/shard_map/all_gather | solution.py:23
  171.6 13.0 %gather_fusion = bf16[16,512,1024]{2,1,0:T(8,128)(2,1)} fusion(bf16[16,512,1024]{2,1,0:T(8,128)(2,1)} %bitcast.3, s32[1024]{0:T(1024)S(1)} %pad_clamp_fusion.1), kind=kCustom, calls=%fused_computation | custom fusion | bytes 33554496 | tf_op jit(solution)/shard_map/gather | solution.py:25
  184.7 13.0 %gather_fusion.1 = bf16[16,512,1024]{2,1,0:T(8,128)(2,1)} fusion(bf16[16,512,1024]{2,1,0:T(8,128)(2,1)} %bitcast.4, s32[1024]{0:T(1024)S(1)} %pad_clamp_fusion), kind=kCustom, calls=%fused_computation.1 | custom fusion | bytes 33554496 | tf_op jit(solution)/shard_map/gather | solution.py:26
  197.7 21.4 %fusion = f32[16,512,512]{2,1,0:T(8,128)} fusion(bf16[16,512,1024]{2,1,0:T(8,128)(2,1)} %gather_fusion, bf16[16,512,1024]{2,1,0:T(8,128)(2,1)} %gather_fusion.1), kind=kOutput, calls=%fused_computation.12 | convolution fusion | flops 8589934592 | bytes 50331648 | tf_op jit(solution)/shard_map/krv,kcv->krc/dot_general | solution.py:32
  219.1 0.0 copy-start
  219.1 0.0 reduce-scatter.2.cloned.1.call-update
  219.1 0.6 copy-done
  219.7 0.1 dynamic-slice_compare_fusion
  219.8 186.7 %reduce-scatter.2.cloned.1.call-done = f32[8,512,512]{2,1,0:T(8,128)} async-done(((f32[16,512,512]{2,1,0:T(8,128)}), f32[8,512,512]{2,1,0:T(8,128)}) %reduce-scatter.2.cloned.1.call-update) | async-done | bytes 8388624 | tf_op jit(solution)/shard_map/reduce_scatter | solution.py:31
  406.5 8.5 %multiply_select_fusion = f32[8,512,512]{2,1,0:T(8,128)} fusion(f32[8,512,512]{2,1,0:T(8,128)} %reduce-scatter.2.cloned.1.call-done, pred[8]{0:T(512)(128)(4,1)S(1)} %dynamic-slice_compare_fusion), kind=kLoop, calls=%fused_computation.2 | loop fusion | flops 4194304 | bytes 16777224 | tf_op jit(solution)/shard_map/jit(_where)/select_n | solution.py:37
  (2 shorter events, 0.0 us)
Async XLA Ops:
  7.2 164.5 %all-gather.2.cloned.1.call-start = ((), (), s32[]{:S(2)}) async-start(), calls=%async_computation.1 | async-start | bytes 17825792 | tf_op jit(solution)/shard_map/all_gather | solution.py:23
  47.3 359.1 %reduce-scatter.2.cloned.1.call-start = ((), (), s32[]{:S(2)}) async-start(), calls=%async_computation.2 | async-start | bytes 25165824 | tf_op jit(solution)/shard_map/reduce_scatter | solution.py:31
  219.1 0.7 copy-start
Sparse Core Ops, SparseCore 0:
  47.5 124.1 all-gather.1
  219.2 187.1 reduce-scatter.1
where the time goes:
time: 422 us
  waiting for transfers between devices  310 us (73%)
  blocking collectives  34.9 us (8%)
  local copies, waits for them, and re-layouts  26.7 us (6%)
  matrix products  21.4 us (5%)
  other arithmetic  15.1 us (4%)
  between operations  14 us (3%)
    reduce_scatter x1, waiting for transfers between devices, per_device(): lax.psum_scatter(jnp.einsum('krv,kcv->krc', row_blocks, col_blocks, prefe...  187 us
    all_gather x1, waiting for transfers between devices, per_device(): gathered = lax.all_gather(standard, 'ind', axis=0, tiled=True)  123 us
    psum x1, blocking collectives, standardize(): total_sum = lax.psum(local_sum, 'ind')  34.9 us
    dot_general x1, matrix products, per_device(): jnp.einsum('krv,kcv->krc', row_blocks, col_blocks, preferred_element_type...  21.4 us
    gather x1, local copies, waits for them, and re-layouts, per_device(): row_blocks = groups[jnp.maximum(tile_rows, 0)]  13 us
    gather x1, local copies, waits for them, and re-layouts, per_device(): col_blocks = groups[jnp.maximum(tile_cols, 0)]  13 us
    select_n x1, other arithmetic, per_device(): jnp.where(listed[:, None, None], summed / VARIANTS, jnp.float32(0.0))  8.53 us
  transfers between devices with their start and end apart: 2, of which 2 were waited for; matrix products, arithmetic and copies ran while one was open for 0% of the time, Pallas kernels for 0%

commit v1 on v0

v1 whole, which is shorter than its diff:
```python
import functools

import jax
import jax.numpy as jnp
from jax import lax
from jax.experimental import pallas as pl
from jax.experimental.pallas import tpu as pltpu
from jax.sharding import PartitionSpec as P

MESH = pl.DeviceIdType.MESH
PIECES = 4
AHEAD = 4


def frequencies(total, people):
    allele_freq = total / (2.0 * people)
    spread = jnp.maximum(2.0 * allele_freq * (1.0 - allele_freq), 0.05)
    return allele_freq, spread


def gather_kernel(
    n, dosages_ref, freq_ref, blocks_ref,
    sums, own, sum_send, sum_recv, local_sem,
    x_send, y_send, up_send, down_send, core_send, column_recv, x_recv, y_recv, diag_recv, core_recv,
):
    rows, variants = own.shape
    zs = n // 4
    piece_rows = rows // PIECES
    me, x = lax.axis_index("ind"), lax.axis_index("slab")
    core, y, z = lax.rem(me, 2), lax.rem(me // 2, 2), me // 4

    def ind_of(z_, y_, core_):
        return (z_ * 2 + y_) * 2 + core_

    to_x = (me, 1 - x)
    to_y = (ind_of(z, 1 - y, core), x)
    to_core = (ind_of(z, y, 1 - core), x)
    to_up = (ind_of(jnp.minimum(z + 1, zs - 1), y, core), x)
    to_down = (ind_of(jnp.maximum(z - 1, 0), y, core), x)

    barrier = pltpu.get_barrier_semaphore()
    pl.semaphore_signal(barrier, inc=1, device_id=to_x, device_id_type=MESH)

    @pl.loop(1, n)
    def _(k):
        other = lax.rem(me + k, n)
        pl.semaphore_signal(barrier, inc=1, device_id=(other, x), device_id_type=MESH)

    sums[pl.ds(me, 1)] = jnp.sum(dosages_ref[...], axis=0).reshape(1, 1, variants)
    pl.semaphore_wait(barrier, n)

    def sum_copy(k, slot):
        other = lax.rem(me + k, n)
        return pltpu.make_async_remote_copy(
            src_ref=sums.at[slot], dst_ref=sums.at[slot],
            send_sem=sum_send.at[k], recv_sem=sum_recv.at[slot],
            device_id=(other, x), device_id_type=MESH,
        )

    @pl.loop(1, n)
    def _(k):
        sum_copy(k, me).start()

    @pl.loop(1, n)
    def _(k):
        sum_copy(k, lax.rem(me + k, n)).wait_recv()

    allele_freq, spread = frequencies(jnp.sum(sums[...], axis=0), rows * n)
    freq_ref[...] = allele_freq
    own[...] = ((dosages_ref[...] - 2.0 * allele_freq) * lax.rsqrt(spread)).astype(jnp.bfloat16)
    keep = pltpu.make_async_copy(own, blocks_ref.at[core, x, z * 2 + y], local_sem)
    keep.start()
    keep.wait()

    @pl.loop(1, n)
    def _(k):
        sum_copy(k, me).wait_send()

    def copy(x_, y_, z_, p, send_sem, recv_sem, to):
        part = blocks_ref.at[core, x_, z_ * 2 + y_, pl.ds(pl.multiple_of(p * piece_rows, piece_rows), piece_rows)]
        return pltpu.make_async_remote_copy(
            src_ref=part, dst_ref=part, send_sem=send_sem, recv_sem=recv_sem,
            device_id=to, device_id_type=MESH,
        )

    def hand_on(x_, y_, z_, p):
        copy(x_, y_, z_, p, core_send, core_recv, to_core).start()

    def nearest(step):
        near = jnp.minimum(z, zs - 1 - z)
        hop = (step + 1) // 2
        close = jnp.where(lax.rem(step, 2) == 1, z - hop, z + hop)
        far = jnp.where(z <= zs - 1 - z, step, zs - 1 - step)
        return jnp.where(step <= 2 * near, close, far)

    def from_column(i):
        z_, p = nearest(i // PIECES), lax.rem(i, PIECES)

        @pl.when(z_ != z)
        def _():
            copy(x, y, z_, p, x_send, column_recv.at[z_, p], to_x).wait_recv()

        @pl.when((z_ <= z) & (z < zs - 1))
        def _():
            copy(x, y, z_, p, up_send, column_recv.at[z_, p], to_up).start()

        @pl.when((z_ >= z) & (z > 0))
        def _():
            copy(x, y, z_, p, down_send, column_recv.at[z_, p], to_down).start()

        copy(x, y, z_, p, x_send, x_recv.at[z_, p], to_x).start()
        copy(x, y, z_, p, y_send, y_recv.at[z_, p], to_y).start()
        hand_on(x, y, z_, p)

    def from_plane(i):
        z_, p = nearest(i // PIECES), lax.rem(i, PIECES)
        copy(1 - x, y, z_, p, x_send, x_recv.at[z_, p], to_x).wait_recv()

        @pl.when(lax.rem(p, 2) == 0)
        def _():
            copy(1 - x, y, z_, p, y_send, diag_recv.at[z_, p], to_y).start()

        hand_on(1 - x, y, z_, p)
        copy(x, 1 - y, z_, p, y_send, y_recv.at[z_, p], to_y).wait_recv()

        @pl.when(lax.rem(p, 2) == 1)
        def _():
            copy(x, 1 - y, z_, p, x_send, diag_recv.at[z_, p], to_x).start()

        hand_on(x, 1 - y, z_, p)

    def from_diagonal(i):
        z_, p = nearest(i // PIECES), lax.rem(i, PIECES)
        copy(1 - x, 1 - y, z_, p, x_send, diag_recv.at[z_, p], to_x).wait_recv()
        hand_on(1 - x, 1 - y, z_, p)

    count = zs * PIECES

    @pl.loop(0, count + 2 * AHEAD)
    def _(i):
        @pl.when(i < count)
        def _():
            from_column(i)

        @pl.when((i >= AHEAD) & (i < count + AHEAD))
        def _():
            from_plane(i - AHEAD)

        @pl.when(i >= 2 * AHEAD)
        def _():
            from_diagonal(i - 2 * AHEAD)

    def drain(sem, blocks):
        view = blocks_ref.at[0, 0, pl.ds(0, blocks)]
        pltpu.make_async_copy(view, view, sem).wait()

    drain(x_send, zs + zs // 2)
    drain(y_send, zs + zs // 2)
    for at in range(zs):
        @pl.when(z == at)
        def _():
            if at < zs - 1:
                drain(up_send, at + 1)
            if at > 0:
                drain(down_send, zs - at)

    half = blocks_ref.at[0]
    pltpu.make_async_copy(half, half, core_send).wait()
    pltpu.make_async_copy(half, half, core_recv).wait()


def tile_kernel(rows_ref, cols_ref, row_block, col_block, out_ref):
    t = pl.program_id(0)
    slabs, variants = row_block.shape[1], row_block.shape[4]

    @pl.when(rows_ref[t] >= 0)
    def _():
        total = None
        for s in range(slabs):
            part = lax.dot_general(
                row_block[0, s, 0], col_block[0, s, 0], (((1,), (1,)), ((), ())),
                preferred_element_type=jnp.float32,
            )
            total = part if total is None else total + part
        out_ref[0] = total / (slabs * variants)

    @pl.when(rows_ref[t] < 0)
    def _():
        out_ref[...] = jnp.zeros_like(out_ref)


def fast(n, slabs, dosages, tile_rows, tile_cols):
    rows, variants = dosages.shape
    zs = n // 4
    dma = pltpu.SemaphoreType.DMA
    allele_freq, blocks = pl.pallas_call(
        functools.partial(gather_kernel, n),
        out_shape=(
            jax.ShapeDtypeStruct((1, variants), jnp.float32),
            jax.ShapeDtypeStruct((2, slabs, n // 2, rows, variants), jnp.bfloat16),
        ),
        in_specs=[pl.BlockSpec(memory_space=pltpu.VMEM)],
        out_specs=(pl.BlockSpec(memory_space=pltpu.VMEM), pl.BlockSpec(memory_space=pl.ANY)),
        scratch_shapes=[
            pltpu.VMEM((n, 1, variants), jnp.float32),
            pltpu.VMEM((rows, variants), jnp.bfloat16),
            dma((n,)), dma((n,)), dma,
            dma, dma, dma, dma, dma,
            dma((zs, PIECES)), dma((zs, PIECES)), dma((zs, PIECES)), dma((zs, PIECES)), dma,
        ],
        compiler_params=pltpu.CompilerParams(
            collective_id=0, has_side_effects=True, vmem_limit_bytes=32 * 1024 * 1024
        ),
    )(dosages)
    per_slab = tile_rows.shape[0] // slabs
    first = lax.axis_index("slab") * per_slab
    own_rows = lax.dynamic_slice_in_dim(tile_rows, first, per_slab, 0)
    own_cols = lax.dynamic_slice_in_dim(tile_cols, first, per_slab, 0)

    def place(t, rows_ref, cols_ref, which):
        block = jnp.maximum((rows_ref, cols_ref)[which][t], 0)
        return (lax.rem(block, 2), 0, block // 2, 0, 0)

    spec = lambda which: pl.BlockSpec(
        (1, slabs, 1, rows, variants), functools.partial(place, which=which)
    )
    grm_tiles = pl.pallas_call(
        tile_kernel,
        out_shape=jax.ShapeDtypeStruct((per_slab, rows, rows), jnp.float32),
        grid_spec=pltpu.PrefetchScalarGridSpec(
            num_scalar_prefetch=2,
            grid=(per_slab,),
            in_specs=[spec(0), spec(1)],
            out_specs=pl.BlockSpec((1, rows, rows), lambda t, r, c: (t, 0, 0)),
        ),
        compiler_params=pltpu.CompilerParams(vmem_limit_bytes=32 * 1024 * 1024),
    )(own_rows, own_cols, blocks, blocks)
    return allele_freq.reshape(variants), grm_tiles


def general(n, slabs, dosages, tile_rows, tile_cols):
    rows, variants = dosages.shape
    allele_freq, spread = frequencies(lax.psum(jnp.sum(dosages, axis=0), "ind"), rows * n)
    standard = ((dosages - 2.0 * allele_freq) * lax.rsqrt(spread)).astype(jnp.bfloat16)
    groups = lax.all_gather(standard, "ind", axis=0)
    row_blocks = groups[jnp.maximum(tile_rows, 0)]
    col_blocks = groups[jnp.maximum(tile_cols, 0)]
    per_slab = tile_rows.shape[0] // slabs
    first = lax.axis_index("slab") * per_slab
    listed = lax.dynamic_slice_in_dim(tile_rows, first, per_slab, 0) >= 0
    summed = lax.psum_scatter(
        jnp.einsum("krv,kcv->krc", row_blocks, col_blocks, preferred_element_type=jnp.float32),
        "slab", scatter_dimension=0, tiled=True,
    )
    return allele_freq, jnp.where(listed[:, None, None], summed / (variants * slabs), jnp.float32(0.0))


def solution(mesh):
    n, slabs = mesh.shape["ind"], mesh.shape["slab"]
    body = fast if slabs == 2 and n % 4 == 0 else general
    in_specs = (P("ind", "slab"), P("ind"), P("ind"))
    out_specs = (P("slab"), P(("ind", "slab"), None, None))
    return jax.shard_map(
        functools.partial(body, n, slabs),
        mesh=mesh, in_specs=in_specs, out_specs=out_specs, check_vma=False,
    )
```

time: 422 us -> 174 us (0.41)
  waiting for transfers between devices: 310 us -> 0 us
  Pallas kernels: 0 us -> 170 us
  blocking collectives: 34.9 us -> 0 us
  local copies, waits for them, and re-layouts: 26.7 us -> 3.64 us
  matrix products: 21.4 us -> 0 us
  other arithmetic: 15.1 us -> 0 us
  between operations: 14 us -> 0.64 us
    reduce_scatter x1 -> x0, waiting for transfers between devices: 187 us -> none  [per_device(): lax.psum_scatter(jnp.einsum('krv,kcv->krc', row_blocks, col_blocks, prefe...]
    pallas_call x0 -> x2, Pallas kernels: none -> 170 us  [the longest x1 151 us: fast(): pl.pallas_call(functools.partial(gather_kernel, n), out_shape=(jax.ShapeD...]
    all_gather x1 -> x0, waiting for transfers between devices: 123 us -> none  [per_device(): gathered = lax.all_gather(standard, 'ind', axis=0, tiled=True)]
    psum x1 -> x0, blocking collectives: 34.9 us -> none  [standardize(): total_sum = lax.psum(local_sum, 'ind')]
    gather x2 -> x0, local copies, waits for them, and re-layouts: 26 us -> none  [the longest x1 13 us: per_device(): row_blocks = groups[jnp.maximum(tile_rows, 0)]]
    dot_general x1 -> x0, matrix products: 21.4 us -> none  [per_device(): jnp.einsum('krv,kcv->krc', row_blocks, col_blocks, preferred_element_type...]
    select_n x1 -> x0, other arithmetic: 8.53 us -> none  [per_device(): jnp.where(listed[:, None, None], summed / VARIANTS, jnp.float32(0.0))]
  transfers between devices with their start and end apart: 2 -> 0, of which waited for: 2 -> 0; matrix products, arithmetic and copies ran while one was open for 0% -> 0% of each run, Pallas kernels for 0% -> 0%
where the time goes in v1:
time: 174 us
  Pallas kernels  170 us (98%)
  local copies, waits for them, and re-layouts  3.64 us (2%)
    pallas_call x1, Pallas kernels, fast(): pl.pallas_call(functools.partial(gather_kernel, n), out_shape=(jax.ShapeD...  151 us
    pallas_call x1, Pallas kernels, fast(): pl.pallas_call(tile_kernel, out_shape=jax.ShapeDtypeStruct((per_slab, row...  19.3 us

profile of v1, /device:TPU:0, one launch (start us, length us, event | category | flops | bytes accessed | tf_op | source)
XLA Modules:
  0.0 174.1 jit_solution(9547408686276382056)
XLA Ops:
  0.6 0.7 dynamic_slice.6.rows_ref
  1.4 0.7 dynamic_slice.7.cols_ref
  2.1 0.0 copy-start
  2.1 1.6 copy-done
  3.7 150.5 %shard_map.50 = (f32[1,1024]{1,0:T(1,128)S(1)}, bf16[2,2,8,512,1024]{4,3,2,1,0:T(8,128)(2,1)}) custom-call(f32[512,1024]{1,0:T(8,128)S(1)} %copy-done), custom_call_target="tpu_custom_call" | custom-call | tf_op jit(solution)/shard_map/pallas_call | solution.py:196
  154.2 19.3 %shard_map.51 = f32[8,512,512]{2,1,0:T(8,128)} custom-call(s32[8]{0:T(128)S(1)} %dynamic_slice.6.rows_ref, s32[8]{0:T(128)S(1)} %dynamic_slice.7.cols_ref, bf16[2,2,8,512,1024]{4,3,2,1,0:T(8,128)(2,1)} %get-tuple-element.5.row_block.col_block, bf16[2,2,8,512,1024]{4,3,2,1,0:T(8,128)(2,1)} %get-tuple-element.5.row_block.col_block), custom_call_target="tpu_custom_call" | custom-call | tf_op jit(solution)/shard_map/pallas_call | solution.py:227
  173.5 0.6 copy.6
Async XLA Ops:
  2.1 1.6 copy-start

commit v2 on v1

v2 whole, which is shorter than its diff:
```python
import functools

import jax
import jax.numpy as jnp
from jax import lax
from jax.experimental import pallas as pl
from jax.experimental.pallas import tpu as pltpu
from jax.sharding import PartitionSpec as P

MESH = pl.DeviceIdType.MESH
PIECES = 8
TURNED = 2
AHEAD = 6


def frequencies(total, people):
    allele_freq = total / (2.0 * people)
    spread = jnp.maximum(2.0 * allele_freq * (1.0 - allele_freq), 0.05)
    return allele_freq, spread


def gather_kernel(
    n, dosages_ref, freq_ref, blocks_ref,
    sums, own, sum_send, sum_recv, local_sem,
    x_send, y_send, up_send, down_send, core_send, recv, core_recv,
):
    rows, variants = own.shape
    zs = n // 4
    piece_rows = rows // PIECES
    me, x = lax.axis_index("ind"), lax.axis_index("slab")
    core, y, z = lax.rem(me, 2), lax.rem(me // 2, 2), me // 4

    def ind_of(z_, y_, core_):
        return (z_ * 2 + y_) * 2 + core_

    to_x = (me, 1 - x)
    to_y = (ind_of(z, 1 - y, core), x)
    to_core = (ind_of(z, y, 1 - core), x)
    to_up = (ind_of(jnp.minimum(z + 1, zs - 1), y, core), x)
    to_down = (ind_of(jnp.maximum(z - 1, 0), y, core), x)

    barrier = pltpu.get_barrier_semaphore()
    pl.semaphore_signal(barrier, inc=1, device_id=to_x, device_id_type=MESH)

    @pl.loop(1, n)
    def _(k):
        other = lax.rem(me + k, n)
        pl.semaphore_signal(barrier, inc=1, device_id=(other, x), device_id_type=MESH)

    sums[pl.ds(me, 1)] = jnp.sum(dosages_ref[...], axis=0).reshape(1, 1, variants)
    pl.semaphore_wait(barrier, n)

    def sum_copy(k, slot):
        other = lax.rem(me + k, n)
        return pltpu.make_async_remote_copy(
            src_ref=sums.at[slot], dst_ref=sums.at[slot],
            send_sem=sum_send.at[k], recv_sem=sum_recv.at[slot],
            device_id=(other, x), device_id_type=MESH,
        )

    @pl.loop(1, n)
    def _(k):
        sum_copy(k, me).start()

    @pl.loop(1, n)
    def _(k):
        sum_copy(k, lax.rem(me + k, n)).wait_recv()

    allele_freq, spread = frequencies(jnp.sum(sums[...], axis=0), rows * n)
    freq_ref[...] = allele_freq
    own[...] = ((dosages_ref[...] - 2.0 * allele_freq) * lax.rsqrt(spread)).astype(jnp.bfloat16)
    at = pl.multiple_of((z * 2 + y) * rows, rows)
    keep = pltpu.make_async_copy(own, blocks_ref.at[core, x, pl.ds(at, rows)], local_sem)
    keep.start()
    keep.wait()

    @pl.loop(1, n)
    def _(k):
        sum_copy(k, me).wait_send()

    def copy(x_, y_, z_, p, send_sem, to):
        at = pl.multiple_of(((z_ * 2 + y_) * PIECES + p) * piece_rows, piece_rows)
        part = blocks_ref.at[core, x_, pl.ds(at, piece_rows)]
        return pltpu.make_async_remote_copy(
            src_ref=part, dst_ref=part, send_sem=send_sem, recv_sem=recv.at[x_ * 2 + y_, z_, p],
            device_id=to, device_id_type=MESH,
        )

    def arrived(x_, y_, z_, p):
        copy(x_, y_, z_, p, x_send, to_x).wait_recv()

    def hand_on(x_, y_, z_, p):
        at = pl.multiple_of(((z_ * 2 + y_) * PIECES + p) * piece_rows, piece_rows)
        part = blocks_ref.at[core, x_, pl.ds(at, piece_rows)]
        pltpu.make_async_remote_copy(
            src_ref=part, dst_ref=part, send_sem=core_send, recv_sem=core_recv,
            device_id=to_core, device_id_type=MESH,
        ).start()

    def along_z(x_, y_, z_, p):
        @pl.when((z_ <= z) & (z < zs - 1))
        def _():
            copy(x_, y_, z_, p, up_send, to_up).start()

        @pl.when((z_ >= z) & (z > 0))
        def _():
            copy(x_, y_, z_, p, down_send, to_down).start()

    def nearest(step):
        near = jnp.minimum(z, zs - 1 - z)
        hop = (step + 1) // 2
        close = jnp.where(lax.rem(step, 2) == 1, z - hop, z + hop)
        far = jnp.where(z <= zs - 1 - z, step, zs - 1 - step)
        return jnp.where(step <= 2 * near, close, far)

    straight = PIECES - TURNED

    def from_column(i):
        z_, p = nearest(i // straight), lax.rem(i, straight)

        @pl.when(z_ != z)
        def _():
            arrived(x, y, z_, p)

        along_z(x, y, z_, p)
        copy(x, y, z_, p, x_send, to_x).start()
        copy(x, y, z_, p, y_send, to_y).start()
        hand_on(x, y, z_, p)

    def from_x(z_, p):
        arrived(1 - x, y, z_, p)

        @pl.when(lax.rem(p, 2) == 0)
        def _():
            copy(1 - x, y, z_, p, y_send, to_y).start()

    def from_y(z_, p):
        arrived(x, 1 - y, z_, p)

        @pl.when(lax.rem(p, 2) == 1)
        def _():
            copy(x, 1 - y, z_, p, x_send, to_x).start()

    def from_plane(i):
        z_, p = nearest(i // straight), lax.rem(i, straight)
        from_x(z_, p)
        hand_on(1 - x, y, z_, p)
        from_y(z_, p)
        hand_on(x, 1 - y, z_, p)

    def from_diagonal(i):
        z_, p = nearest(i // straight), lax.rem(i, straight)
        arrived(1 - x, 1 - y, z_, p)
        hand_on(1 - x, 1 - y, z_, p)

    def from_turned(j):
        z_, k, p = nearest(j // (4 * TURNED)), lax.rem(j // TURNED, 4), straight + lax.rem(j, TURNED)
        x_ = lax.rem(x + lax.rem(k, 2), 2)
        y_ = lax.rem(y + k // 2, 2)

        @pl.when((z_ == z) & (k == 1))
        def _():
            from_x(z, p)

        @pl.when((z_ == z) & (k == 2))
        def _():
            from_y(z, p)

        @pl.when((z_ != z) | (k == 3))
        def _():
            arrived(x_, y_, z_, p)

        along_z(x_, y_, z_, p)
        hand_on(x_, y_, z_, p)

    @pl.loop(straight, PIECES)
    def _(p):
        copy(x, y, z, p, x_send, to_x).start()
        copy(x, y, z, p, y_send, to_y).start()

    count = zs * straight
    turned = 4 * zs * TURNED

    @pl.loop(0, count + 2 * AHEAD)
    def _(i):
        @pl.when(i < count)
        def _():
            from_column(i)

        k = i - AHEAD

        @pl.when((k >= 0) & (k < count))
        def _():
            @pl.loop(k * turned // count, (k + 1) * turned // count)
            def _(j):
                from_turned(j)

            from_plane(k)

        @pl.when(i >= 2 * AHEAD)
        def _():
            from_diagonal(i - 2 * AHEAD)

    def drain(sem, pieces):
        view = blocks_ref.at[0, 0, pl.ds(0, pieces * piece_rows)]
        pltpu.make_async_copy(view, view, sem).wait()

    over = (zs * straight + TURNED) * 3 // 2
    drain(x_send, over)
    drain(y_send, over)
    for at in range(zs):
        @pl.when(z == at)
        def _():
            if at < zs - 1:
                drain(up_send, (at + 1) * (straight + 4 * TURNED))
            if at > 0:
                drain(down_send, (zs - at) * (straight + 4 * TURNED))

    half = blocks_ref.at[0]
    pltpu.make_async_copy(half, half, core_send).wait()
    pltpu.make_async_copy(half, half, core_recv).wait()


def tile_kernel(all_variants, rows_ref, cols_ref, row_block, col_block, out_ref):
    t = pl.program_id(0)

    @pl.when(rows_ref[t] >= 0)
    def _():
        total = None
        for s in range(row_block.shape[1]):
            part = lax.dot_general(
                row_block[0, s, 0], col_block[0, s, 0], (((1,), (1,)), ((), ())),
                preferred_element_type=jnp.float32,
            )
            total = part if total is None else total + part
        out_ref[0] = total / all_variants

    @pl.when(rows_ref[t] < 0)
    def _():
        out_ref[...] = jnp.zeros_like(out_ref)


def tiles(all_variants, blocks, tile_rows, tile_cols):
    cores, slabs, _, rows, variants = blocks.shape
    count = tile_rows.shape[0]

    def place(t, rows_ref, cols_ref, which):
        block = jnp.maximum((rows_ref, cols_ref)[which][t], 0)
        return (lax.rem(block, cores), 0, block // cores, 0, 0)

    spec = lambda which: pl.BlockSpec(
        (1, slabs, 1, rows, variants), functools.partial(place, which=which)
    )
    return pl.pallas_call(
        functools.partial(tile_kernel, all_variants),
        out_shape=jax.ShapeDtypeStruct((count, rows, rows), jnp.float32),
        grid_spec=pltpu.PrefetchScalarGridSpec(
            num_scalar_prefetch=2,
            grid=(count,),
            in_specs=[spec(0), spec(1)],
            out_specs=pl.BlockSpec((1, rows, rows), lambda t, r, c: (t, 0, 0)),
        ),
        compiler_params=pltpu.CompilerParams(vmem_limit_bytes=32 * 1024 * 1024),
    )(tile_rows, tile_cols, blocks, blocks)


def fast(n, slabs, dosages, tile_rows, tile_cols):
    rows, variants = dosages.shape
    zs = n // 4
    dma = pltpu.SemaphoreType.DMA
    allele_freq, blocks = pl.pallas_call(
        functools.partial(gather_kernel, n),
        out_shape=(
            jax.ShapeDtypeStruct((1, variants), jnp.float32),
            jax.ShapeDtypeStruct((2, slabs, n // 2 * rows, variants), jnp.bfloat16),
        ),
        in_specs=[pl.BlockSpec(memory_space=pltpu.VMEM)],
        out_specs=(pl.BlockSpec(memory_space=pltpu.VMEM), pl.BlockSpec(memory_space=pl.ANY)),
        scratch_shapes=[
            pltpu.VMEM((n, 1, variants), jnp.float32),
            pltpu.VMEM((rows, variants), jnp.bfloat16),
            dma((n,)), dma((n,)), dma,
            dma, dma, dma, dma, dma,
            dma((2 * slabs, zs, PIECES)), dma,
        ],
        compiler_params=pltpu.CompilerParams(
            collective_id=0, has_side_effects=True, vmem_limit_bytes=32 * 1024 * 1024
        ),
    )(dosages)
    per_slab = tile_rows.shape[0] // slabs
    first = lax.axis_index("slab") * per_slab
    own_rows = lax.dynamic_slice_in_dim(tile_rows, first, per_slab, 0)
    own_cols = lax.dynamic_slice_in_dim(tile_cols, first, per_slab, 0)

    grm_tiles = tiles(variants * slabs, blocks.reshape(2, slabs, n // 2, rows, variants), own_rows, own_cols)
    return allele_freq.reshape(variants), grm_tiles


def general(n, slabs, dosages, tile_rows, tile_cols):
    rows, variants = dosages.shape
    allele_freq, spread = frequencies(lax.psum(jnp.sum(dosages, axis=0), "ind"), rows * n)
    standard = ((dosages - 2.0 * allele_freq) * lax.rsqrt(spread)).astype(jnp.bfloat16)
    groups = lax.all_gather(standard, "ind", axis=0)
    shares = tiles(variants * slabs, groups[None, None], tile_rows, tile_cols)
    return allele_freq, lax.psum_scatter(shares, "slab", scatter_dimension=0, tiled=True)


def solution(mesh):
    n, slabs = mesh.shape["ind"], mesh.shape["slab"]
    body = fast if slabs == 2 and n % 4 == 0 else general
    in_specs = (P("ind", "slab"), P("ind"), P("ind"))
    out_specs = (P("slab"), P(("ind", "slab"), None, None))
    return jax.shard_map(
        functools.partial(body, n, slabs),
        mesh=mesh, in_specs=in_specs, out_specs=out_specs, check_vma=False,
    )
```

time: 174 us -> 171 us (0.983)
  Pallas kernels: 170 us -> 165 us
    pallas_call x1, Pallas kernels: 151 us -> 148 us  [fast(): pl.pallas_call(functools.partial(gather_kernel, n), out_shape=(jax.ShapeD...]
where the time goes in v2:
time: 171 us; the launch traced here: 170 us
  Pallas kernels  165 us (96%)
  local copies, waits for them, and re-layouts  3.64 us (2%)
    pallas_call x1, Pallas kernels, fast(): pl.pallas_call(functools.partial(gather_kernel, n), out_shape=(jax.ShapeD...  148 us
    pallas_call x1, Pallas kernels, tiles(): pl.pallas_call(functools.partial(tile_kernel, all_variants), out_shape=ja...  17.6 us

profile of v2, /device:TPU:0, one launch (start us, length us, event | category | flops | bytes accessed | tf_op | source)
XLA Modules:
  0.0 169.6 jit_solution(11588843924748602956)
XLA Ops:
  0.6 0.7 dynamic_slice.6.rows_ref
  1.4 0.7 dynamic_slice.7.cols_ref
  2.1 0.0 copy-start
  2.1 1.6 copy-done
  3.7 147.7 %shard_map.50 = (f32[1,1024]{1,0:T(1,128)S(1)}, bf16[2,2,4096,1024]{3,2,1,0:T(8,128)(2,1)}) custom-call(f32[512,1024]{1,0:T(8,128)S(1)} %copy-done), custom_call_target="tpu_custom_call" | custom-call | tf_op jit(solution)/shard_map/pallas_call | solution.py:271
  151.4 17.6 %shard_map.51 = f32[8,512,512]{2,1,0:T(8,128)} custom-call(s32[8]{0:T(128)S(1)} %dynamic_slice.6.rows_ref, s32[8]{0:T(128)S(1)} %dynamic_slice.7.cols_ref, bf16[2,2,8,512,1024]{4,3,2,1,0:T(8,128)(2,1)} %bitcast.3, bf16[2,2,8,512,1024]{4,3,2,1,0:T(8,128)(2,1)} %bitcast.4), custom_call_target="tpu_custom_call" | custom-call | tf_op jit(solution)/shard_map/pallas_call | solution.py:254
  169.0 0.6 copy.6
Async XLA Ops:
  2.1 1.6 copy-start

commit v3 on v2

--- a/solution.py
+++ b/solution.py
@@ -10,7 +10,8 @@
 MESH = pl.DeviceIdType.MESH
 PIECES = 8
 TURNED = 2
-AHEAD = 6
+AHEAD = 3
+LATE = 10
 
 
 def frequencies(total, people):
@@ -106,27 +107,57 @@
         def _():
             copy(x_, y_, z_, p, down_send, to_down).start()
 
-    def nearest(step):
-        near = jnp.minimum(z, zs - 1 - z)
-        hop = (step + 1) // 2
-        close = jnp.where(lax.rem(step, 2) == 1, z - hop, z + hop)
-        far = jnp.where(z <= zs - 1 - z, step, zs - 1 - step)
-        return jnp.where(step <= 2 * near, close, far)
-
     straight = PIECES - TURNED
-
-    def from_column(i):
-        z_, p = nearest(i // straight), lax.rem(i, straight)
-
-        @pl.when(z_ != z)
-        def _():
-            arrived(x, y, z_, p)
-
+    count = zs * straight
+    first = (zs - 1) * straight
+    slots = first + (zs - 1) * 4 * TURNED
+
+    def nth(i):
+        m = i - straight
+        both = jnp.minimum(z, zs - 1 - z) * 2 * straight
+        q = lax.rem(m, 2 * straight)
+        hop = m // (2 * straight) + 1
+        near = jnp.where(lax.rem(q, 2) == 0, z - hop, z + hop)
+        rest = m - both
+        hop = jnp.minimum(z, zs - 1 - z) + 1 + rest // straight
+        far = jnp.where(z <= zs - 1 - z, z + hop, z - hop)
+        z_ = jnp.where(m < 0, z, jnp.where(m < both, near, far))
+        p = jnp.where(m < 0, i, jnp.where(m < both, q // 2, lax.rem(rest, straight)))
+        return z_, p
+
+    def straight_on(z_, p):
         along_z(x, y, z_, p)
         copy(x, y, z_, p, x_send, to_x).start()
         copy(x, y, z_, p, y_send, to_y).start()
         hand_on(x, y, z_, p)
 
+    def corner(j):
+        k = lax.rem(j // TURNED, 4)
+        return lax.rem(x + lax.rem(k, 2), 2), lax.rem(y + k // 2, 2), straight + lax.rem(j, TURNED)
+
+    def along(k, sign):
+        @pl.when(k < first)
+        def _():
+            z_ = z + sign * (k // straight + 1)
+
+            @pl.when((z_ >= 0) & (z_ < zs))
+            def _():
+                p = lax.rem(k, straight)
+                arrived(x, y, z_, p)
+                straight_on(z_, p)
+
+        @pl.when(k >= first)
+        def _():
+            j = k - first
+            z_ = z + sign * (j // (4 * TURNED) + 1)
+
+            @pl.when((z_ >= 0) & (z_ < zs))
+            def _():
+                x_, y_, p = corner(j)
+                arrived(x_, y_, z_, p)
+                along_z(x_, y_, z_, p)
+                hand_on(x_, y_, z_, p)
+
     def from_x(z_, p):
         arrived(1 - x, y, z_, p)
 
@@ -142,64 +173,70 @@
             copy(x, 1 - y, z_, p, x_send, to_x).start()
 
     def from_plane(i):
-        z_, p = nearest(i // straight), lax.rem(i, straight)
+        z_, p = nth(i)
         from_x(z_, p)
         hand_on(1 - x, y, z_, p)
         from_y(z_, p)
         hand_on(x, 1 - y, z_, p)
 
     def from_diagonal(i):
-        z_, p = nearest(i // straight), lax.rem(i, straight)
+        z_, p = nth(i)
         arrived(1 - x, 1 - y, z_, p)
         hand_on(1 - x, 1 - y, z_, p)
-
-    def from_turned(j):
-        z_, k, p = nearest(j // (4 * TURNED)), lax.rem(j // TURNED, 4), straight + lax.rem(j, TURNED)
-        x_ = lax.rem(x + lax.rem(k, 2), 2)
-        y_ = lax.rem(y + k // 2, 2)
-
-        @pl.when((z_ == z) & (k == 1))
-        def _():
-            from_x(z, p)
-
-        @pl.when((z_ == z) & (k == 2))
-        def _():
-            from_y(z, p)
-
-        @pl.when((z_ != z) | (k == 3))
-        def _():
-            arrived(x_, y_, z_, p)
-
-        along_z(x_, y_, z_, p)
-        hand_on(x_, y_, z_, p)
 
     @pl.loop(straight, PIECES)
     def _(p):
         copy(x, y, z, p, x_send, to_x).start()
         copy(x, y, z, p, y_send, to_y).start()
 
-    count = zs * straight
-    turned = 4 * zs * TURNED
-
-    @pl.loop(0, count + 2 * AHEAD)
+    @pl.loop(0, straight)
+    def _(p):
+        straight_on(z, p)
+
+    @pl.loop(0, count + LATE)
     def _(i):
-        @pl.when(i < count)
-        def _():
-            from_column(i)
-
-        k = i - AHEAD
-
-        @pl.when((k >= 0) & (k < count))
-        def _():
-            @pl.loop(k * turned // count, (k + 1) * turned // count)
-            def _(j):
-                from_turned(j)
-
-            from_plane(k)
-
-        @pl.when(i >= 2 * AHEAD)
-        def _():
-            from_diagonal(i - 2 * AHEAD)
+        now = jnp.minimum(i, count)
+        later = jnp.minimum(i + 1, count)
+
+        @pl.loop(now * slots // count, later * slots // count)
+        def _(k):
+            along(k, -1)
+            along(k, 1)
+
+            @pl.when(k == first // 2)
+            def _():
+                @pl.loop(0, 4 * TURNED)
+                def _(j):
+                    x_, y_, p = corner(j)
+
+                    @pl.when(j // TURNED == 1)
+                    def _():
+                        from_x(z, p)
+
+                    @pl.when(j // TURNED == 2)
+                    def _():
+                        from_y(z, p)
+
+            @pl.when(k == first - TURNED)
+            def _():
+                @pl.loop(0, 4 * TURNED)
+                def _(j):
+                    x_, y_, p = corner(j)
+
+                    @pl.when(j // TURNED == 3)
+                    def _():
+                        arrived(x_, y_, z, p)
+
+                    along_z(x_, y_, z, p)
+                    hand_on(x_, y_, z, p)
+
+        @pl.when((i >= AHEAD) & (i < count + AHEAD))
+        def _():
+            from_plane(i - AHEAD)
+
+        @pl.when(i >= LATE)
+        def _():
+            from_diagonal(i - LATE)
 
     def drain(sem, pieces):
         view = blocks_ref.at[0, 0, pl.ds(0, pieces * piece_rows)]

time: 171 us -> 171 us (level)
  Pallas kernels: 165 us -> 167 us
where the time goes in v3:
time: 171 us
  Pallas kernels  167 us (98%)
  local copies, waits for them, and re-layouts  3.64 us (2%)
    pallas_call x1, Pallas kernels, fast(): pl.pallas_call(functools.partial(gather_kernel, n), out_shape=(jax.ShapeD...  148 us
    pallas_call x1, Pallas kernels, tiles(): pl.pallas_call(functools.partial(tile_kernel, all_variants), out_shape=ja...  19.1 us

profile of v3, /device:TPU:0, one launch (start us, length us, event | category | flops | bytes accessed | tf_op | source)
XLA Modules:
  0.0 171.1 jit_solution(453030193802332601)
XLA Ops:
  0.6 0.7 dynamic_slice.6.rows_ref
  1.4 0.7 dynamic_slice.7.cols_ref
  2.1 0.0 copy-start
  2.1 1.6 copy-done
  3.7 147.7 %shard_map.50 = (f32[1,1024]{1,0:T(1,128)S(1)}, bf16[2,2,4096,1024]{3,2,1,0:T(8,128)(2,1)}) custom-call(f32[512,1024]{1,0:T(8,128)S(1)} %copy-done), custom_call_target="tpu_custom_call" | custom-call | tf_op jit(solution)/shard_map/pallas_call | solution.py:308
  151.4 19.1 %shard_map.51 = f32[8,512,512]{2,1,0:T(8,128)} custom-call(s32[8]{0:T(128)S(1)} %dynamic_slice.6.rows_ref, s32[8]{0:T(128)S(1)} %dynamic_slice.7.cols_ref, bf16[2,2,8,512,1024]{4,3,2,1,0:T(8,128)(2,1)} %bitcast.3, bf16[2,2,8,512,1024]{4,3,2,1,0:T(8,128)(2,1)} %bitcast.4), custom_call_target="tpu_custom_call" | custom-call | tf_op jit(solution)/shard_map/pallas_call | solution.py:291
  170.5 0.6 copy.6
Async XLA Ops:
  2.1 1.6 copy-start

commit v4 on v3

--- a/solution.py
+++ b/solution.py
@@ -8,10 +8,10 @@
 from jax.sharding import PartitionSpec as P
 
 MESH = pl.DeviceIdType.MESH
-PIECES = 8
+PIECES = 16
 TURNED = 2
-AHEAD = 3
-LATE = 10
+AHEAD = 6
+LATE = 20
 
 
 def frequencies(total, people):

time: 171 us -> 168 us (0.982)
  Pallas kernels: 167 us -> 163 us
    pallas_call x1, Pallas kernels: 148 us -> 144 us  [fast(): pl.pallas_call(functools.partial(gather_kernel, n), out_shape=(jax.ShapeD...]
where the time goes in v4:
time: 168 us
  Pallas kernels  163 us (97%)
  local copies, waits for them, and re-layouts  3.64 us (2%)
    pallas_call x1, Pallas kernels, fast(): pl.pallas_call(functools.partial(gather_kernel, n), out_shape=(jax.ShapeD...  144 us
    pallas_call x1, Pallas kernels, tiles(): pl.pallas_call(functools.partial(tile_kernel, all_variants), out_shape=ja...  19.3 us

profile of v4, /device:TPU:0, one launch (start us, length us, event | category | flops | bytes accessed | tf_op | source)
XLA Modules:
  0.0 167.7 jit_solution(6177987919883761169)
XLA Ops:
  0.6 0.7 dynamic_slice.6.rows_ref
  1.4 0.7 dynamic_slice.7.cols_ref
  2.1 0.0 copy-start
  2.1 1.6 copy-done
  3.7 144.1 %shard_map.50 = (f32[1,1024]{1,0:T(1,128)S(1)}, bf16[2,2,4096,1024]{3,2,1,0:T(8,128)(2,1)}) custom-call(f32[512,1024]{1,0:T(8,128)S(1)} %copy-done), custom_call_target="tpu_custom_call" | custom-call | tf_op jit(solution)/shard_map/pallas_call | solution.py:308
  147.8 19.3 %shard_map.51 = f32[8,512,512]{2,1,0:T(8,128)} custom-call(s32[8]{0:T(128)S(1)} %dynamic_slice.6.rows_ref, s32[8]{0:T(128)S(1)} %dynamic_slice.7.cols_ref, bf16[2,2,8,512,1024]{4,3,2,1,0:T(8,128)(2,1)} %bitcast.3, bf16[2,2,8,512,1024]{4,3,2,1,0:T(8,128)(2,1)} %bitcast.4), custom_call_target="tpu_custom_call" | custom-call | tf_op jit(solution)/shard_map/pallas_call | solution.py:291
  167.1 0.6 copy.6
Async XLA Ops:
  2.1 1.6 copy-start

commit v5 on v4

--- a/solution.py
+++ b/solution.py
@@ -21,8 +21,8 @@
 
 
 def gather_kernel(
-    n, dosages_ref, freq_ref, blocks_ref,
-    sums, own, sum_send, sum_recv, local_sem,
+    n, given_ref, freq_ref, blocks_ref,
+    dosages_ref, sums, own, sum_send, sum_recv, local_sem,
     x_send, y_send, up_send, down_send, core_send, recv, core_recv,
 ):
     rows, variants = own.shape
@@ -40,6 +40,8 @@
     to_up = (ind_of(jnp.minimum(z + 1, zs - 1), y, core), x)
     to_down = (ind_of(jnp.maximum(z - 1, 0), y, core), x)
 
+    fetch = pltpu.make_async_copy(given_ref, dosages_ref, local_sem)
+    fetch.start()
     barrier = pltpu.get_barrier_semaphore()
     pl.semaphore_signal(barrier, inc=1, device_id=to_x, device_id_type=MESH)
 
@@ -48,6 +50,7 @@
         other = lax.rem(me + k, n)
         pl.semaphore_signal(barrier, inc=1, device_id=(other, x), device_id_type=MESH)
 
+    fetch.wait()
     sums[pl.ds(me, 1)] = jnp.sum(dosages_ref[...], axis=0).reshape(1, 1, variants)
     pl.semaphore_wait(barrier, n)
 
@@ -311,9 +314,10 @@
             jax.ShapeDtypeStruct((1, variants), jnp.float32),
             jax.ShapeDtypeStruct((2, slabs, n // 2 * rows, variants), jnp.bfloat16),
         ),
-        in_specs=[pl.BlockSpec(memory_space=pltpu.VMEM)],
+        in_specs=[pl.BlockSpec(memory_space=pl.ANY)],
         out_specs=(pl.BlockSpec(memory_space=pltpu.VMEM), pl.BlockSpec(memory_space=pl.ANY)),
         scratch_shapes=[
+            pltpu.VMEM((rows, variants), jnp.float32),
             pltpu.VMEM((n, 1, variants), jnp.float32),
             pltpu.VMEM((rows, variants), jnp.bfloat16),
             dma((n,)), dma((n,)), dma,
@@ -321,7 +325,7 @@
             dma((2 * slabs, zs, PIECES)), dma,
         ],
         compiler_params=pltpu.CompilerParams(
-            collective_id=0, has_side_effects=True, vmem_limit_bytes=32 * 1024 * 1024
+            collective_id=0, has_side_effects=True, vmem_limit_bytes=60 * 1024 * 1024
         ),
     )(dosages)
     per_slab = tile_rows.shape[0] // slabs

time: 168 us -> 167 us (level)
  the two profiles are of different devices: /device:TPU:0 before, /device:TPU:1 now
where the time goes in v5:
time: 167 us; the launch traced here: 166 us
  Pallas kernels  163 us (98%)
  local copies, waits for them, and re-layouts  2.06 us (1%)
    pallas_call x1, Pallas kernels, fast(): pl.pallas_call(functools.partial(gather_kernel, n), out_shape=(jax.ShapeD...  145 us
    pallas_call x1, Pallas kernels, tiles(): pl.pallas_call(functools.partial(tile_kernel, all_variants), out_shape=ja...  18.6 us

profile of v5, /device:TPU:1, one launch (start us, length us, event | category | flops | bytes accessed | tf_op | source)
XLA Modules:
  0.0 166.1 jit_solution(4602635397616261748)
XLA Ops:
  0.6 0.7 dynamic_slice.6.rows_ref
  1.4 0.7 dynamic_slice.7.cols_ref
  2.1 144.8 %shard_map.50 = (f32[1,1024]{1,0:T(1,128)}, bf16[2,2,4096,1024]{3,2,1,0:T(8,128)(2,1)}) custom-call(f32[512,1024]{1,0:T(8,128)} %given_ref.1), custom_call_target="tpu_custom_call" | custom-call | tf_op jit(solution)/shard_map/pallas_call | solution.py:311
  146.9 0.0 copy-start
  146.9 18.6 %shard_map.51 = f32[8,512,512]{2,1,0:T(8,128)} custom-call(s32[8]{0:T(128)S(1)} %dynamic_slice.6.rows_ref, s32[8]{0:T(128)S(1)} %dynamic_slice.7.cols_ref, bf16[2,2,8,512,1024]{4,3,2,1,0:T(8,128)(2,1)} %bitcast.2, bf16[2,2,8,512,1024]{4,3,2,1,0:T(8,128)(2,1)} %bitcast.3), custom_call_target="tpu_custom_call" | custom-call | tf_op jit(solution)/shard_map/pallas_call | solution.py:294
  165.5 0.0 copy-done
  165.5 0.6 copy.6
Async XLA Ops:
  146.9 18.6 %copy-start = (f32[1,1024]{1,0:T(1,128)S(1)}, f32[1,1024]{1,0:T(1,128)}, u32[]{:S(2)}) copy-start(f32[1,1024]{1,0:T(1,128)} %get-tuple-element.4) | copy-start | bytes 12292
